TPU v7x, 128 devices: a whole 4x4x4 slice. The times are simulated.
128 devices in a mesh: ex: 8 (over z, core), feat: 16 (over y, x).
Axes of the slice: x: 4, y: 4, z: 4, core: 2. Of those that a mesh axis runs over, the one named last changes fastest.
Arguments:
- lengths: int32 [2048], P(('ex', 'feat')), may hold values from 1 to 32, 40960 in all
- attn_in: bfloat16 [2048, 32, 4096], P(('ex', 'feat')), may hold values from -6 to 6
- context: bfloat16 [2048, 32, 4096], P(('ex', 'feat')), may hold values from -6 to 6
- grad_q: bfloat16 [2048, 32, 4096], P(('ex', 'feat')), may hold values from -6 to 6
- grad_k: bfloat16 [2048, 32, 1024], P(('ex', 'feat')), may hold values from -6 to 6
- grad_v: bfloat16 [2048, 32, 1024], P(('ex', 'feat')), may hold values from -6 to 6
- grad_o: bfloat16 [2048, 32, 4096], P(('ex', 'feat')), may hold values from -6 to 6
- proj_in: bfloat16 [4, 64, 4096], replicated, may hold values from -0.09375 to 0.09375
- proj_out_wide: bfloat16 [2, 64, 4096], replicated, may hold values from -0.09375 to 0.09375
- proj_out_narrow: bfloat16 [2, 64, 1024], replicated, may hold values from -0.1875 to 0.1875
- inv_hessian: float32 [4, 16, 256, 256], P(None, 'feat'), as said below
- query_feats: float32 [256, 4, 4096], P('ex', None, 'feat'), may hold values from -6 to 6
Outputs:
- scores: float32 [2048, 256], P(('ex', 'feat'))
Inputs may be any that keep to these rules, and one draw needn't show every extreme that they name: `lengths`: each example's count of real tokens; some example has exactly 32. `inv_hessian`: each block is symmetric, and in each row the magnitudes off the diagonal sum to less than the diagonal entry.
All inputs are finite; a program needn't handle non-finite values. No bound on the sum of `lengths` on one device may be relied on, other than what follows from the above.
Results may differ from a plain program's by a relative error of at most 0.0041.
Values may be sent and summed in bfloat16 or wider, within the bound.
A program may use at most 128 MiB of HBM per device.

v0:
```python
import jax
import jax.numpy as jnp
from jax import lax
from jax.sharding import PartitionSpec as P

PR = 64
FM = 4096
HB = 256
LEN = 32


def per_device(
    lengths,
    attn_in,
    context,
    grad_q,
    grad_k,
    grad_v,
    grad_o,
    proj_in,
    proj_out_wide,
    proj_out_narrow,
    inv_hessian,
    query_feats,
):
    owners = lax.axis_size("feat")
    count = lengths.shape[0]
    group_rows = count * owners
    share = FM // owners
    positions = jnp.arange(LEN, dtype=jnp.int32)
    keep = (positions[None, :] < lengths[:, None]).astype(jnp.float32)[:, :, None]
    sources = (attn_in, attn_in, attn_in, context)
    targets = (grad_q, grad_k, grad_v, grad_o)
    outside = (proj_out_wide[0], proj_out_narrow[0], proj_out_narrow[1], proj_out_wide[1])
    received = []
    for matrix in range(4):
        source = sources[matrix].reshape(count * LEN, -1)
        target = targets[matrix].reshape(count * LEN, -1)
        in_proj = jnp.dot(source, proj_in[matrix].T, preferred_element_type=jnp.float32).reshape(
            count, LEN, PR
        )
        out_proj = jnp.dot(target, outside[matrix].T, preferred_element_type=jnp.float32).reshape(
            count, LEN, PR
        )
        outer_in_proj = (in_proj * keep).astype(jnp.bfloat16)
        outer_out_proj = (out_proj * keep).astype(jnp.bfloat16)
        grads = jnp.einsum(
            "eti,etj->eij", outer_out_proj, outer_in_proj, preferred_element_type=jnp.float32
        )
        received.append(
            lax.all_to_all(
                grads.reshape(count, FM), "feat", split_axis=1, concat_axis=0, tiled=True
            )
        )
    regrouped = jnp.stack(received, axis=1)
    blocks = share // HB
    precond = jnp.einsum(
        "rmkf,mkfg->rmkg",
        regrouped.reshape(group_rows, 4, blocks, HB),
        inv_hessian,
        precision=lax.Precision.HIGHEST,
    )
    precond = precond.reshape(group_rows, 4 * share)
    self_part = jnp.sum(precond * regrouped.reshape(group_rows, 4 * share), axis=1)
    piece = lax.all_gather(query_feats, "ex", axis=0, tiled=True)
    partial_value = jnp.dot(
        precond, piece.reshape(piece.shape[0], 4 * share).T, precision=lax.Precision.HIGHEST
    )
    self_total = lax.psum(self_part, "feat")
    scaled = partial_value * lax.rsqrt(self_total + 1e-06)[:, None]
    scores = lax.psum_scatter(scaled, "feat", scatter_dimension=0, tiled=True)
    return scores


def solution(mesh):
    in_specs = (
        P(("ex", "feat")),
        P(("ex", "feat"), None, None),
        P(("ex", "feat"), None, None),
        P(("ex", "feat"), None, None),
        P(("ex", "feat"), None, None),
        P(("ex", "feat"), None, None),
        P(("ex", "feat"), None, None),
        P(),
        P(),
        P(),
        P(None, "feat", None, None),
        P("ex", None, "feat"),
    )
    out_specs = P(("ex", "feat"), None)
    return jax.shard_map(
        per_device, mesh=mesh, in_specs=in_specs, out_specs=out_specs, check_vma=False
    )
```

profile of v0, /device:TPU:1, one launch (start us, length us, event | category | flops | bytes accessed | tf_op | source)
XLA Modules:
  0.0 191.9 jit_solution(4112335083751592582)
XLA Ops:
  6.5 0.0 copy-start
  6.5 0.0 copy-start.1
  6.5 0.0 copy-start.3
  6.5 0.9 fusion.42
  7.4 3.5 %fusion.2 = bf16[16,32,64]{2,1,0:T(8,128)(2,1)S(1)} fusion(bf16[16,32,4096]{2,1,0:T(8,128)(2,1)} %param.13, bf16[4,64,4096]{2,1,0:T(8,128)(2,1)} %param.19, f32[16,32]{1,0:T(8,128)S(1)} %fusion.42), kind=kOutput, calls=%fused_computation.12 | convolution fusion | flops 268500992 | bytes 4786176 | tf_op jit(solution)/shard_map/dot_general | solution.py:39
  11.0 0.0 copy-done.1
  11.0 0.0 copy-done.3
  11.0 0.7 fusion.9
  11.7 0.0 copy-start.2
  11.7 0.2 all_to_all.51
  11.9 0.9 copy.27
  12.8 7.6 %all-to-all-start.1 = ((f32[16,16,256]{2,0,1:T(8,128)}), f32[16,16,256]{2,0,1:T(8,128)S(1)}, u32[]{:S(2)}, u32[]{:S(2)}) async-start(f32[16,16,256]{2,0,1:T(8,128)} %copy.27), calls=%async_computation.1 | async-start | bytes 524288 | tf_op jit(solution)/shard_map/all_to_all | solution.py:51
  20.4 0.0 all-gather.2.cloned.1.call-start
  20.4 0.7 all-gather.2.cloned.1.call-update
  21.1 3.5 %fusion.3 = bf16[16,32,64]{2,1,0:T(8,128)(2,1)S(1)} fusion(bf16[16,32,4096]{2,1,0:T(8,128)(2,1)} %param.13, bf16[4,64,4096]{2,1,0:T(8,128)(2,1)} %param.19, f32[16,32]{1,0:T(8,128)S(1)} %fusion.42), kind=kOutput, calls=%fused_computation.13 | convolution fusion | flops 268500992 | bytes 4786176 | tf_op jit(solution)/shard_map/dot_general | solution.py:39
  24.7 0.0 copy-done.2
  24.7 0.7 fusion.8
  25.4 0.2 all_to_all.54
  25.6 0.9 copy.28
  26.4 3.5 %fusion = bf16[16,32,64]{2,1,0:T(8,128)(2,1)S(1)} fusion(bf16[16,32,4096]{2,1,0:T(8,128)(2,1)} %param.15, bf16[2,64,4096]{2,1,0:T(8,128)(2,1)} %param.20, f32[16,32]{1,0:T(8,128)S(1)} %fusion.42), kind=kOutput, calls=%fused_computation.10 | convolution fusion | flops 268500992 | bytes 4786176 | tf_op jit(solution)/shard_map/dot_general | solution.py:42
  30.0 0.0 copy-start.4
  30.0 3.8 %fusion.11 = f32[16,64,64]{2,1,0:T(8,128)S(1)} fusion(bf16[16,32,64]{2,1,0:T(8,128)(2,1)S(1)} %fusion, bf16[16,32,4096]{2,1,0:T(8,128)(2,1)} %param.13, bf16[4,64,4096]{2,1,0:T(8,128)(2,1)} %param.19, f32[16,32]{1,0:T(8,128)S(1)} %fusion.42), kind=kOutput, calls=%fused_computation.21 | convolution fusion | flops 272695296 | bytes 5048320 | tf_op jit(solution)/shard_map/eti,etj->eij/dot_general | solution.py:47
  33.8 0.2 all_to_all.48
  34.0 0.9 copy.26
  34.9 0.0 all-to-all-done.1
  34.9 6.6 %all-to-all-start.2 = ((f32[16,16,256]{2,0,1:T(8,128)}), f32[16,16,256]{2,0,1:T(8,128)S(1)}, u32[]{:S(2)}, u32[]{:S(2)}) async-start(f32[16,16,256]{2,0,1:T(8,128)} %copy.28), calls=%async_computation.2 | async-start | bytes 524288 | tf_op jit(solution)/shard_map/all_to_all | solution.py:51
  41.5 0.0 copy-done.4
  41.5 3.5 %fusion.4 = bf16[16,32,64]{2,1,0:T(8,128)(2,1)S(1)} fusion(bf16[16,32,4096]{2,1,0:T(8,128)(2,1)} %param.18, bf16[2,64,4096]{2,1,0:T(8,128)(2,1)S(1)} %copy-done.4, f32[16,32]{1,0:T(8,128)S(1)} %fusion.42), kind=kOutput, calls=%fused_computation.14 | convolution fusion | flops 268500992 | bytes 4792320 | tf_op jit(solution)/shard_map/dot_general | solution.py:42
  45.0 4.0 %all-to-all-done.2 = f32[16,16,256]{2,0,1:T(8,128)S(1)} async-done(((f32[16,16,256]{2,0,1:T(8,128)}), f32[16,16,256]{2,0,1:T(8,128)S(1)}, u32[]{:S(2)}, u32[]{:S(2)}) %all-to-all-start.2) | async-done | bytes 262176 | tf_op jit(solution)/shard_map/all_to_all | solution.py:51
  49.1 3.5 %all-to-all-start = ((f32[16,16,256]{2,0,1:T(8,128)}), f32[16,16,256]{2,0,1:T(8,128)S(1)}, u32[]{:S(2)}, u32[]{:S(2)}) async-start(f32[16,16,256]{2,0,1:T(8,128)} %copy.26), calls=%async_computation | async-start | bytes 524288 | tf_op jit(solution)/shard_map/all_to_all | solution.py:51
  52.6 0.0 reduce-scatter.2.cloned.1.call-start
  52.6 3.7 %fusion.10 = f32[16,64,64]{2,1,0:T(8,128)S(1)} fusion(bf16[16,32,64]{2,1,0:T(8,128)(2,1)S(1)} %fusion.4, bf16[16,32,4096]{2,1,0:T(8,128)(2,1)} %param.14, bf16[4,64,4096]{2,1,0:T(8,128)(2,1)} %param.19, f32[16,32]{1,0:T(8,128)S(1)} %fusion.42), kind=kOutput, calls=%fused_computation.20 | convolution fusion | flops 272695296 | bytes 5048320 | tf_op jit(solution)/shard_map/eti,etj->eij/dot_general | solution.py:47
  56.4 0.2 all_to_all.57
  56.6 0.2 copy.29
  56.7 3.5 %all-to-all-done = f32[16,16,256]{2,0,1:T(8,128)S(1)} async-done(((f32[16,16,256]{2,0,1:T(8,128)}), f32[16,16,256]{2,0,1:T(8,128)S(1)}, u32[]{:S(2)}, u32[]{:S(2)}) %all-to-all-start) | async-done | bytes 262176 | tf_op jit(solution)/shard_map/all_to_all | solution.py:51
  60.2 10.5 %all_to_all.64 = f32[16,16,256]{2,0,1:T(8,128)S(1)} all-to-all(f32[16,16,256]{2,0,1:T(8,128)S(1)} %copy.29), channel_id=1, replica_groups=mesh['ex'=8,'feat'=16] {'feat'}, dimensions={1} | all-to-all | bytes 524288 | tf_op jit(solution)/shard_map/all_to_all | solution.py:51
  70.7 0.0 copy-done
  70.7 1.3 fusion.12
  72.0 0.3 copy.32
  72.3 29.8 %psum.7 = f32[256]{0:T(256)S(1)} all-reduce(f32[256]{0:T(256)S(1)} %get-tuple-element.5), channel_id=1, replica_groups=mesh['ex'=8,'feat'=16] {'feat'}, use_global_device_ids=true, to_apply=%region_1.0 | all-reduce | flops 256 | bytes 2048 | tf_op jit(solution)/shard_map/psum | solution.py:69
  102.1 0.0 all-gather.2.cloned.1.call-done
  102.1 1.4 copy.35
  103.6 2.5 %convolution_multiply_fusion.6 = f32[256,256]{1,0:T(8,128)} fusion(f32[256,1024]{0,1:T(8,128)S(1)} %bitcast.80, f32[256,1024]{1,0:T(8,128)S(1)} %bitcast.81, f32[256]{0:T(256)S(1)} %add_rsqrt_fusion), kind=kOutput, calls=%fused_computation.7 | convolution fusion | flops 805371904 | bytes 2360320 | tf_op jit(solution)/shard_map/dot_general | solution.py:66
  106.1 0.0 reduce-scatter.2.cloned.1.call-update
  106.1 78.9 %reduce-scatter.2.cloned.1.call-done = f32[16,256]{1,0:T(8,128)} async-done(((f32[256,256]{1,0:T(8,128)}), f32[16,256]{1,0:T(8,128)}) %reduce-scatter.2.cloned.1.call-update) | async-done | bytes 16400 | tf_op jit(solution)/shard_map/reduce_scatter | solution.py:71
  (1 shorter events, 0.0 us)
Async XLA Ops:
  6.5 64.1 %copy-start = (f32[4,1,256,256]{3,2,1,0:T(8,128)S(1)}, f32[4,1,256,256]{3,2,1,0:T(8,128)}, u32[]{:S(2)}) copy-start(f32[4,1,256,256]{3,2,1,0:T(8,128)} %param.22) | copy-start | bytes 3145732
  6.5 4.4 %copy-start.1 = (bf16[16,32,1024]{2,1,0:T(8,128)(2,1)S(1)}, bf16[16,32,1024]{2,1,0:T(8,128)(2,1)}, u32[]{:S(2)}) copy-start(bf16[16,32,1024]{2,1,0:T(8,128)(2,1)} %param.16) | copy-start | bytes 3145732
  6.5 4.4 %copy-start.3 = (bf16[2,64,1024]{2,1,0:T(8,128)(2,1)S(1)}, bf16[2,64,1024]{2,1,0:T(8,128)(2,1)}, u32[]{:S(2)}) copy-start(bf16[2,64,1024]{2,1,0:T(8,128)(2,1)} %param.21) | copy-start | bytes 786436
  11.7 12.9 %copy-start.2 = (bf16[16,32,1024]{2,1,0:T(8,128)(2,1)S(1)}, bf16[16,32,1024]{2,1,0:T(8,128)(2,1)}, u32[]{:S(2)}) copy-start(bf16[16,32,1024]{2,1,0:T(8,128)(2,1)} %param.17) | copy-start | bytes 3145732
  12.8 22.1 %all-to-all-start.1 = ((f32[16,16,256]{2,0,1:T(8,128)}), f32[16,16,256]{2,0,1:T(8,128)S(1)}, u32[]{:S(2)}, u32[]{:S(2)}) async-start(f32[16,16,256]{2,0,1:T(8,128)} %copy.27), calls=%async_computation.1 | async-start | bytes 524288 | tf_op jit(solution)/shard_map/all_to_all | solution.py:51
  20.4 81.8 %all-gather.2.cloned.1.call-start = ((), (), s32[]{:S(2)}) async-start(), calls=%async_computation.5 | async-start | bytes 1179648 | tf_op jit(solution)/shard_map/all_gather | solution.py:65
  30.0 11.5 %copy-start.4 = (bf16[2,64,4096]{2,1,0:T(8,128)(2,1)S(1)}, bf16[2,64,4096]{2,1,0:T(8,128)(2,1)}, u32[]{:S(2)}) copy-start(bf16[2,64,4096]{2,1,0:T(8,128)(2,1)} %param.20) | copy-start | bytes 3145732
  34.9 14.2 %all-to-all-start.2 = ((f32[16,16,256]{2,0,1:T(8,128)}), f32[16,16,256]{2,0,1:T(8,128)S(1)}, u32[]{:S(2)}, u32[]{:S(2)}) async-start(f32[16,16,256]{2,0,1:T(8,128)} %copy.28), calls=%async_computation.2 | async-start | bytes 524288 | tf_op jit(solution)/shard_map/all_to_all | solution.py:51
  49.1 11.1 %all-to-all-start = ((f32[16,16,256]{2,0,1:T(8,128)}), f32[16,16,256]{2,0,1:T(8,128)S(1)}, u32[]{:S(2)}, u32[]{:S(2)}) async-start(f32[16,16,256]{2,0,1:T(8,128)} %copy.26), calls=%async_computation | async-start | bytes 524288 | tf_op jit(solution)/shard_map/all_to_all | solution.py:51
  52.6 132.5 %reduce-scatter.2.cloned.1.call-start = ((), (), s32[]{:S(2)}) async-start(), calls=%async_computation.6 | async-start | bytes 278528 | tf_op jit(solution)/shard_map/reduce_scatter | solution.py:71
Sparse Core Ops, SparseCore 0:
  22.9 26.8 all-gather.1
  106.2 78.7 reduce-scatter.1
where the time goes:
time: 193 us; the launch traced here: 192 us
  waiting for transfers between devices  87.2 us (45%)
  blocking collectives  40.3 us (21%)
  matrix products  27 us (14%)
  starting transfers between devices  17.8 us (9%)
  between operations  13.6 us (7%)
  local copies, waits for them, and re-layouts  5.2 us (3%)
    reduce_scatter x1, waiting for transfers between devices, per_device(): scores = lax.psum_scatter(scaled, 'feat', scatter_dimension=0, tiled=True)  78.9 us
    psum x1, blocking collectives, per_device(): self_total = lax.psum(self_part, 'feat')  29.8 us
    all_to_all x3, starting transfers between devices, per_device(): lax.all_to_all(grads.reshape(count, FM), 'feat', split_axis=1, concat_axi...  17.8 us
    all_to_all x1, blocking collectives, per_device(): lax.all_to_all(grads.reshape(count, FM), 'feat', split_axis=1, concat_axi...  10.5 us
    dot_general x4, matrix products, per_device(): jnp.einsum('eti,etj->eij', outer_out_proj, outer_in_proj, preferred_eleme...  9.05 us
    all_to_all x3, waiting for transfers between devices, per_device(): lax.all_to_all(grads.reshape(count, FM), 'feat', split_axis=1, concat_axi...  7.52 us
    dot_general x2, matrix products, per_device(): jnp.dot(source, proj_in[matrix].T, preferred_element_type=jnp.float32)  7.07 us
    dot_general x2, matrix products, per_device(): jnp.dot(target, outside[matrix].T, preferred_element_type=jnp.float32)  7.03 us
  transfers between devices with their start and end apart: 5, of which 3 were waited for; matrix products, arithmetic and copies ran while one was open for 12% of the time, Pallas kernels for 0%

commit v1 on v0

v1 whole, which is shorter than its diff:
```python
import functools

import jax
import jax.numpy as jnp
from jax import lax
from jax.experimental import pallas as pl
from jax.experimental.pallas import tpu as pltpu
from jax.sharding import PartitionSpec as P

MESH = pl.DeviceIdType.MESH
NT = (((1,), (1,)), ((), ()))
BF = jnp.bfloat16
F32 = jnp.float32

D = 4096
KVW = 1024
PR = 64
HB = 256
LEN = 32
EXD = 16
ROWS = EXD * LEN
OWN = 16
EXN = 8
QL = 32
QN = 256
RC = 256
NC = ROWS // RC
W = 384


def kernel(
    len_ref, xa, xc, gq, gk, gv, go, win, wwide, wnar, hes, qry, out_ref,
    xa_v, xc_v, gq_v, gk_v, gv_v, go_v, win_v, wwide_v, wnar_v, hes_v, qry_v,
    hb_v, ploc, pall, pin, pin_o, ot, mask_v, g32, gsend, grec, acc, tacc, sbuf, srec,
    load_sem, p_send, p_recv, g_send, g_recv, s_send, s_recv,
):
    ex = lax.axis_index("ex")
    ft = lax.axis_index("feat")
    fy, fx = ft // 4, ft % 4

    def peer(s):
        return ((fy + s // 4) % 4) * 4 + (fx + s % 4) % 4

    loads = {}

    def load(name, src, dst):
        copy = pltpu.make_async_copy(src, dst, load_sem.at[len(loads)])
        copy.start()
        loads[name] = copy

    load("hes", hes.at[:, 0], hes_v)
    load("qry", qry, qry_v)
    for m in range(3):
        load(f"win{m}", win.at[m], win_v.at[pl.ds(m * PR, PR)])
    for c in range(NC):
        load(f"xa{c}", xa.at[pl.ds(c * RC, RC)], xa_v.at[pl.ds(c * RC, RC)])
    load("wnar", wnar, wnar_v)
    for c in range(NC):
        load(f"gk{c}", gk.at[pl.ds(c * RC, RC)], gk_v.at[pl.ds(c * RC, RC)])
    for c in range(NC):
        load(f"gv{c}", gv.at[pl.ds(c * RC, RC)], gv_v.at[pl.ds(c * RC, RC)])
    load("wq", wwide.at[0], wwide_v.at[0])
    for c in range(NC):
        load(f"gq{c}", gq.at[pl.ds(c * RC, RC)], gq_v.at[pl.ds(c * RC, RC)])
    load("win3", win.at[3], win_v.at[pl.ds(4 * PR, PR)])
    for c in range(NC):
        load(f"xc{c}", xc.at[pl.ds(c * RC, RC)], xc_v.at[pl.ds(c * RC, RC)])
    load("wo", wwide.at[1], wwide_v.at[1])
    for c in range(NC):
        load(f"go{c}", go.at[pl.ds(c * RC, RC)], go_v.at[pl.ds(c * RC, RC)])

    barrier = pltpu.get_barrier_semaphore()

    @pl.loop(1, OWN)
    def _(s):
        pl.semaphore_signal(barrier, inc=1, device_id={"feat": peer(s)}, device_id_type=MESH)

    @pl.loop(1, EXN)
    def _(s):
        pl.semaphore_signal(barrier, inc=1, device_id={"ex": (ex + s) % EXN}, device_id_type=MESH)

    lane = lax.broadcasted_iota(jnp.int32, (16, 256), 1)
    lane_e = (lane // LEN) % 4
    lane_t = lane % LEN
    for e in range(EXD):
        on = (lane_e == e % 4) & (lane_t < len_ref[e])
        mask_v[e * 16:(e + 1) * 16, :] = jnp.where(on, 1.0, 0.0).astype(BF)

    loads["hes"].wait()
    loads["qry"].wait()
    for m in range(4):
        ploc[m] = jnp.dot(
            qry_v[:, m, :], hes_v[m], preferred_element_type=F32, precision=lax.Precision.HIGHEST
        ).astype(BF)
        hb_v[m] = hes_v[m].astype(BF)

    pl.semaphore_wait(barrier, OWN - 1 + EXN - 1)

    my_q = pl.ds(pl.multiple_of(ex * QL, QL), QL)

    def p_copy(s):
        return pltpu.make_async_remote_copy(
            src_ref=ploc, dst_ref=pall.at[:, my_q, :], send_sem=p_send, recv_sem=p_recv,
            device_id={"ex": (ex + s) % EXN}, device_id_type=MESH,
        )

    @pl.loop(1, EXN)
    def _(s):
        p_copy(s).start()

    pall[:, my_q, :] = ploc[...]

    half = lax.broadcasted_iota(jnp.int32, (128, 128), 1) < PR
    my_rows = pl.ds(pl.multiple_of(ft * EXD, EXD), EXD)

    def rows_of(k):
        return pl.ds(pl.multiple_of(k * EXD, EXD), EXD)

    def g_copy(m, s):
        to = peer(s)
        return pltpu.make_async_remote_copy(
            src_ref=gsend.at[m, rows_of(to), :], dst_ref=grec.at[m, my_rows, :],
            send_sem=g_send.at[m], recv_sem=g_recv.at[m],
            device_id={"feat": to}, device_id_type=MESH,
        )

    def outer(m, c, target_v, weight, pair, dup):
        rows = pl.ds(c * RC, RC)
        o_t = lax.dot_general(weight, target_v[rows, :], NT, preferred_element_type=F32)
        for b in range(RC // 128):
            ot[b] = o_t[:, b * 128:(b + 1) * 128]
        for b in range(RC // 128):
            g = c * (RC // 128) + b
            parts = [
                [ot[b, pl.ds(2 * ih + il, 16, stride=4), :].astype(BF) for il in range(2)]
                for ih in range(2)
            ]
            lhs = jnp.concatenate([jnp.concatenate(p, axis=1) for p in parts], axis=0)
            blocks = []
            for e in range(4):
                mk = mask_v[(4 * g + e) * 16:(4 * g + e + 1) * 16, :]
                blocks.append(lhs * jnp.concatenate([mk, mk], axis=0))
            lhs = jnp.concatenate(blocks, axis=0)
            top, bottom = pair(g)
            rhs = jnp.concatenate([top, bottom], axis=0)
            r = jnp.dot(lhs, rhs, preferred_element_type=F32)
            for e in range(4):
                for ih in range(2):
                    at = (2 * e + ih) * 16
                    g32[ih, pl.ds(4 * g + e, 16, stride=16), :] = r[at:at + 16, :]

    def finish(m):
        gsend[m] = jnp.concatenate([g32[0], g32[1]], axis=1).astype(BF)

        @pl.loop(1, OWN)
        def _(s):
            g_copy(m, s).start()

        grec[m, my_rows, :] = gsend[m, my_rows, :]

    def split(x, left):
        turned = pltpu.roll(x, PR, axis=1)
        on_left, on_right = (x, turned) if left else (turned, x)
        return jnp.where(half, on_left, 0.0).astype(BF), jnp.where(half, 0.0, on_right).astype(BF)

    def group(g):
        return pl.ds(g * 128, 128)

    for m in range(3):
        loads[f"win{m}"].wait()
    win_v[pl.ds(3 * PR, PR), :] = win_v[pl.ds(2 * PR, PR), :]
    for c in range(NC):
        loads[f"xa{c}"].wait()
        pin[c * RC:(c + 1) * RC, :] = lax.dot_general(
            xa_v[c * RC:(c + 1) * RC, :], win_v[0:4 * PR, :], NT, preferred_element_type=F32
        )

    def pair_q(g):
        return split(pin[group(g), 0:128], True)

    def pair_k(g):
        return split(pin[group(g), 0:128], False)

    def pair_v(g):
        x = pin[group(g), 128:256]
        return jnp.where(half, x, 0.0).astype(BF), jnp.where(half, 0.0, x).astype(BF)

    def pair_o(g):
        x = pin_o[group(g), :]
        return jnp.where(half, x, 0.0).astype(BF), jnp.where(half, 0.0, x).astype(BF)

    loads["wnar"].wait()
    for c in range(NC):
        loads[f"gk{c}"].wait()
        outer(1, c, gk_v, wnar_v[0], pair_k, False)
    finish(1)
    for c in range(NC):
        loads[f"gv{c}"].wait()
        outer(2, c, gv_v, wnar_v[1], pair_v, True)
    finish(2)
    loads["wq"].wait()
    for c in range(NC):
        loads[f"gq{c}"].wait()
        outer(0, c, gq_v, wwide_v[0], pair_q, False)
    finish(0)
    loads["win3"].wait()
    win_v[pl.ds(5 * PR, PR), :] = win_v[pl.ds(4 * PR, PR), :]
    for c in range(NC):
        loads[f"xc{c}"].wait()
        pin_o[c * RC:(c + 1) * RC, :] = lax.dot_general(
            xc_v[c * RC:(c + 1) * RC, :], win_v[4 * PR:6 * PR, :], NT, preferred_element_type=F32
        )
    loads["wo"].wait()
    for c in range(NC):
        loads[f"go{c}"].wait()
        outer(3, c, go_v, wwide_v[1], pair_o, True)
    finish(3)

    others = (OWN - 1) * EXD
    pltpu.make_async_copy(
        pall.at[:, pl.ds(0, QN - QL), :], pall.at[:, pl.ds(0, QN - QL), :], p_recv
    ).wait()
    order = (1, 2, 0, 3)
    for i, m in enumerate(order):
        pltpu.make_async_copy(
            grec.at[m, pl.ds(0, others), :], grec.at[m, pl.ds(0, others), :], g_recv.at[m]
        ).wait()
        got = grec[m]
        raw = lax.dot_general(got, pall[m], NT, preferred_element_type=F32)
        own = jnp.dot(got, hb_v[m], preferred_element_type=F32) * got.astype(F32)
        own = own[:, 0:128] + own[:, 128:256]
        if i == 0:
            acc[...] = raw
            tacc[...] = own
        elif i < 3:
            acc[...] += raw
            tacc[...] += own
        else:
            raw = acc[...] + raw
            own = tacc[...] + own
            own = own + pltpu.roll(own, 64, axis=1)
            high = own.astype(BF).astype(F32)
            lanes = lax.broadcasted_iota(jnp.int32, (OWN * EXD, 128), 1)
            own = jnp.where(lanes < 64, high, own - high)
            sbuf[:, 0:QN] = raw.astype(BF)
            sbuf[:, QN:W] = own.astype(BF)

    def s_copy(s):
        to = peer(s)
        return pltpu.make_async_remote_copy(
            src_ref=sbuf.at[rows_of(to), :], dst_ref=srec.at[my_rows, :],
            send_sem=s_send, recv_sem=s_recv, device_id={"feat": to}, device_id_type=MESH,
        )

    @pl.loop(1, OWN)
    def _(s):
        s_copy(s).start()

    srec[my_rows, :] = sbuf[my_rows, :]
    pltpu.make_async_copy(
        srec.at[pl.ds(0, others), :], srec.at[pl.ds(0, others), :], s_recv
    ).wait()
    total = srec[0:EXD, :].astype(F32)
    for s in range(1, OWN):
        total = total + srec[s * EXD:(s + 1) * EXD, :].astype(F32)
    self_inf = jnp.sum(total[:, QN:W], axis=1, keepdims=True)
    out_ref[...] = total[:, 0:QN] * lax.rsqrt(self_inf + 1e-06)

    for m in range(4):
        pltpu.make_async_copy(
            gsend.at[m, pl.ds(0, others), :], gsend.at[m, pl.ds(0, others), :], g_send.at[m]
        ).wait()
    pltpu.make_async_copy(
        sbuf.at[pl.ds(0, others), :], sbuf.at[pl.ds(0, others), :], s_send
    ).wait()
    pltpu.make_async_copy(
        pall.at[:, pl.ds(0, QN - QL), :], pall.at[:, pl.ds(0, QN - QL), :], p_send
    ).wait()


def per_device(
    lengths, attn_in, context, grad_q, grad_k, grad_v, grad_o,
    proj_in, proj_out_wide, proj_out_narrow, inv_hessian, query_feats,
):
    def flat(x):
        return x.reshape(ROWS, x.shape[-1])

    any_space = pl.BlockSpec(memory_space=pl.ANY)
    dma = pltpu.SemaphoreType.DMA
    return pl.pallas_call(
        kernel,
        out_shape=jax.ShapeDtypeStruct((EXD, QN), F32),
        in_specs=[pl.BlockSpec(memory_space=pltpu.SMEM)] + [any_space] * 11,
        out_specs=pl.BlockSpec(memory_space=pltpu.VMEM),
        scratch_shapes=[
            pltpu.VMEM((ROWS, D), BF),
            pltpu.VMEM((ROWS, D), BF),
            pltpu.VMEM((ROWS, D), BF),
            pltpu.VMEM((ROWS, KVW), BF),
            pltpu.VMEM((ROWS, KVW), BF),
            pltpu.VMEM((ROWS, D), BF),
            pltpu.VMEM((6 * PR, D), BF),
            pltpu.VMEM((2, PR, D), BF),
            pltpu.VMEM((2, PR, KVW), BF),
            pltpu.VMEM((4, HB, HB), F32),
            pltpu.VMEM((QL, 4, HB), F32),
            pltpu.VMEM((4, HB, HB), BF),
            pltpu.VMEM((4, QL, HB), BF),
            pltpu.VMEM((4, QN, HB), BF),
            pltpu.VMEM((ROWS, 256), F32),
            pltpu.VMEM((ROWS, 128), F32),
            pltpu.VMEM((RC // 128, PR, 128), F32),
            pltpu.VMEM((EXD * 16, 256), BF),
            pltpu.VMEM((2, OWN * EXD, 128), F32),
            pltpu.VMEM((4, OWN * EXD, HB), BF),
            pltpu.VMEM((4, OWN * EXD, HB), BF),
            pltpu.VMEM((OWN * EXD, QN), F32),
            pltpu.VMEM((OWN * EXD, 128), F32),
            pltpu.VMEM((OWN * EXD, W), BF),
            pltpu.VMEM((OWN * EXD, W), BF),
            dma((40,)),
            dma,
            dma,
            dma((4,)),
            dma((4,)),
            dma,
            dma,
        ],
        compiler_params=pltpu.CompilerParams(
            collective_id=0, has_side_effects=True, vmem_limit_bytes=56 << 20
        ),
    )(
        lengths, flat(attn_in), flat(context), flat(grad_q), flat(grad_k), flat(grad_v),
        flat(grad_o), proj_in, proj_out_wide, proj_out_narrow, inv_hessian, query_feats,
    )


def solution(mesh):
    both = P(("ex", "feat"), None, None)
    in_specs = (
        P(("ex", "feat")), both, both, both, both, both, both,
        P(), P(), P(),
        P(None, "feat", None, None),
        P("ex", None, "feat"),
    )
    return jax.shard_map(
        per_device, mesh=mesh, in_specs=in_specs, out_specs=P(("ex", "feat"), None), check_vma=False
    )
```

time: 193 us -> 34.7 us (0.18)
  waiting for transfers between devices: 87.2 us -> 0 us
  blocking collectives: 40.3 us -> 0 us
  Pallas kernels: 0 us -> 32.9 us
  matrix products: 27 us -> 0 us
  starting transfers between devices: 17.8 us -> 0 us
  between operations: 13.6 us -> 0.01 us
  local copies, waits for them, and re-layouts: 5.2 us -> 1.32 us
    reduce_scatter x1 -> x0, waiting for transfers between devices: 78.9 us -> none  [per_device(): scores = lax.psum_scatter(scaled, 'feat', scatter_dimension=0, tiled=True)]
    pallas_call x0 -> x1, Pallas kernels: none -> 32.9 us  [per_device(): pl.pallas_call(kernel, out_shape=jax.ShapeDtypeStruct((EXD, QN), F32), in...]
    psum x1 -> x0, blocking collectives: 29.8 us -> none  [per_device(): self_total = lax.psum(self_part, 'feat')]
    dot_general x10 -> x0, matrix products: 27 us -> none  [the longest x4 9.05 us: per_device(): jnp.einsum('eti,etj->eij', outer_out_proj, outer_in_proj, preferred_eleme...]
    all_to_all x3 -> x0, starting transfers between devices: 17.8 us -> none  [per_device(): lax.all_to_all(grads.reshape(count, FM), 'feat', split_axis=1, concat_axi...]
    all_to_all x1 -> x0, blocking collectives: 10.5 us -> none  [per_device(): lax.all_to_all(grads.reshape(count, FM), 'feat', split_axis=1, concat_axi...]
    all_to_all x3 -> x0, waiting for transfers between devices: 7.52 us -> none  [per_device(): lax.all_to_all(grads.reshape(count, FM), 'feat', split_axis=1, concat_axi...]
    all_to_all x8 -> x0, local copies, waits for them, and re-layouts: 3.42 us -> none  [per_device(): lax.all_to_all(grads.reshape(count, FM), 'feat', split_axis=1, concat_axi...]
  transfers between devices with their start and end apart: 5 -> 0, of which waited for: 3 -> 0; matrix products, arithmetic and copies ran while one was open for 12% -> 0% of each run, Pallas kernels for 0% -> 0%
where the time goes in v1:
time: 34.7 us; the launch traced here: 34.3 us
  Pallas kernels  32.9 us (95%)
  local copies, waits for them, and re-layouts  1.32 us (4%)
    pallas_call x1, Pallas kernels, per_device(): pl.pallas_call(kernel, out_shape=jax.ShapeDtypeStruct((EXD, QN), F32), in...  32.9 us
    unnamed x1, local copies, waits for them, and re-layouts  1.32 us

profile of v1, /device:TPU:1, one launch (start us, length us, event | category | flops | bytes accessed | tf_op | source)
XLA Modules:
  0.0 34.3 jit_solution(2167638684375398234)
XLA Ops:
  0.0 32.9 %shard_map.118 = f32[16,256]{1,0:T(8,128)} custom-call(s32[16]{0:T(128)} %len_ref.1, bf16[512,4096]{1,0:T(8,128)(2,1)} %bitcast.6, bf16[512,4096]{1,0:T(8,128)(2,1)} %bitcast.7, bf16[512,4096]{1,0:T(8,128)(2,1)} %bitcast.8, bf16[512,1024]{1,0:T(8,128)(2,1)} %bitcast.10, bf16[512,1024]{1,0:T(8,128)(2,1)} %bitcast.11, bf16[512,4096]{1,0:T(8,128)(2,1)} %bitcast.9, ...), custom_call_target="tpu_custom_call" | custom-call | tf_op jit(solution)/shard_map/pallas_call | solution.py:290
  32.9 1.3 %copy.14 = f32[16,256]{1,0:T(8,128)} copy(f32[16,256]{1,0:T(8,128)} %shard_map.118) | data formatting | bytes 32768

commit v2 on v1

v2 whole, which is shorter than its diff:
```python
import jax
import jax.numpy as jnp
from jax import lax
from jax.experimental import pallas as pl
from jax.experimental.pallas import tpu as pltpu
from jax.sharding import PartitionSpec as P

MESH = pl.DeviceIdType.MESH
NT = (((1,), (1,)), ((), ()))
BF = jnp.bfloat16
F32 = jnp.float32

D = 4096
KVW = 1024
PR = 64
HB = 256
LEN = 32
EXD = 16
ROWS = EXD * LEN
SIDE = 4
OWN = SIDE * SIDE
EXN = 8
QL = 32
QN = 256
W = 384
PITCH = 17
QUERY, KEY, VALUE, OUTPUT = range(4)


def hops(s):
    dy, dx = divmod(s, SIDE)
    return min(dy, SIDE - dy) + min(dx, SIDE - dx)


SLOTS = sorted(range(OWN), key=hops)
GROUPS = [[i for i in range(OWN) if max(hops(SLOTS[i]), 1) == h] for h in range(1, SIDE + 1)]
GROUP_OF = {i: n for n, g in enumerate(GROUPS) for i in g}
FAR_FIRST = range(OWN - 1, 0, -1)


def arrived(ref, sem):
    pltpu.make_async_copy(ref, ref, sem).wait()


def kernel(
    len_ref, xa, xc, gq, gk, gv, go, win, wwide, wnar, hes, qry, out_ref,
    xa_v, xc_v, gq_v, gk_v, gv_v, go_v, win_v, wwide_v, wnar_v, hes_v, qry_v,
    hb_v, ploc, pall, pin, pin_o, ot, mask_v, g32, gsend, grec, acc, tacc, sbuf, srec,
    load_sem, p_send, p_recv, g_send, g_recv, s_send, s_recv,
):
    ex = lax.axis_index("ex")
    ft = lax.axis_index("feat")
    fy, fx = ft // SIDE, ft % SIDE

    def ahead(i):
        dy, dx = divmod(SLOTS[i], SIDE)
        return ((fy + dy) % SIDE) * SIDE + (fx + dx) % SIDE

    def behind(i):
        dy, dx = divmod(SLOTS[i], SIDE)
        return ((fy + SIDE - dy) % SIDE) * SIDE + (fx + SIDE - dx) % SIDE

    loads = {}
    waited = set()

    def load(name, src, dst):
        copy = pltpu.make_async_copy(src, dst, load_sem.at[len(loads)])
        copy.start()
        loads[name] = copy

    def ready(*names):
        for name in names:
            loads[name].wait()
            waited.add(name)

    def load_rows(name, src, dst, at, size):
        load(name, src.at[pl.ds(at, size)], dst.at[pl.ds(at, size)])

    load("hes", hes.at[:, 0], hes_v)
    load("qry", qry, qry_v)
    load("wnar", wnar, wnar_v)
    load("gk", gk, gk_v)
    load("gv", gv, gv_v)
    load("win", win.at[pl.ds(0, 3)], win_v.at[pl.ds(0, 3)])
    load_rows("xa0", xa, xa_v, 0, 256)
    load_rows("xa1", xa, xa_v, 256, 256)
    load("wq", wwide.at[0], wwide_v.at[0])
    load_rows("gq0", gq, gq_v, 0, 256)
    load_rows("gq1", gq, gq_v, 256, 256)
    load("win3", win.at[3], win_v.at[4])
    load_rows("xc0", xc, xc_v, 0, 256)
    load_rows("xc1", xc, xc_v, 256, 256)
    load("wo", wwide.at[1], wwide_v.at[1])
    load_rows("go0", go, go_v, 0, 256)
    load_rows("go1", go, go_v, 256, 128)
    load_rows("go2", go, go_v, 384, 128)

    barrier = pltpu.get_barrier_semaphore()
    for i in FAR_FIRST:
        pl.semaphore_signal(barrier, inc=1, device_id={"feat": ahead(i)}, device_id_type=MESH)
    for s in range(1, EXN):
        pl.semaphore_signal(barrier, inc=1, device_id={"ex": (ex + s) % EXN}, device_id_type=MESH)

    lane = lax.broadcasted_iota(jnp.int32, (16, 256), 1)
    lane_e = (lane // LEN) % 4
    lane_t = lane % LEN
    for e in range(EXD):
        on = (lane_e == e % 4) & (lane_t < len_ref[e])
        mask_v[e * 16:(e + 1) * 16, :] = jnp.where(on, 1.0, 0.0).astype(BF)

    def halves(x):
        high = x.astype(BF)
        return high, (x - high.astype(F32)).astype(BF)

    ready("hes", "qry")
    for m in range(4):
        q_high, q_low = halves(qry_v[:, m, :])
        h_high, h_low = halves(hes_v[m])
        hb_v[m] = h_high
        both = jnp.dot(
            jnp.concatenate([q_high, q_low], axis=0), h_high, preferred_element_type=F32
        )
        rest = jnp.dot(q_high, h_low, preferred_element_type=F32)
        ploc[m] = (both[0:QL] + (both[QL:2 * QL] + rest)).astype(BF)

    pl.semaphore_wait(barrier, OWN - 1 + EXN - 1)

    my_q = pl.ds(pl.multiple_of(ex * QL, QL), QL)
    for s in range(1, EXN):
        pltpu.make_async_remote_copy(
            src_ref=ploc, dst_ref=pall.at[:, my_q, :], send_sem=p_send, recv_sem=p_recv,
            device_id={"ex": (ex + s) % EXN}, device_id_type=MESH,
        ).start()
    pall[:, my_q, :] = ploc[...]

    half = lax.broadcasted_iota(jnp.int32, (128, 128), 1) < PR

    def rows_of(k):
        return pl.ds(pl.multiple_of(k * EXD, EXD), EXD)

    def project(m, target_v, weight, first, count):
        o_t = lax.dot_general(
            weight, target_v[first:first + count, :], NT, preferred_element_type=F32
        )
        for b in range(count // 128):
            ot[m, first // 128 + b] = o_t[:, b * 128:(b + 1) * 128]

    def split(x, left, twice):
        turned = x if twice else pltpu.roll(x, PR, axis=1)
        on_left, on_right = (x, turned) if left else (turned, x)
        return jnp.where(half, on_left, 0.0).astype(BF), jnp.where(half, 0.0, on_right).astype(BF)

    def pair(m, g):
        rows = pl.ds(g * 128, 128)
        if m == QUERY:
            return split(pin[rows, 0:128], True, False)
        if m == KEY:
            return split(pin[rows, 0:128], False, False)
        if m == VALUE:
            return split(pin[rows, 128:256], True, True)
        return split(pin_o[rows, :], True, True)

    def outer(m, g):
        parts = [
            [ot[m, g, pl.ds(2 * ih + il, 16, stride=4), :].astype(BF) for il in range(2)]
            for ih in range(2)
        ]
        lhs = jnp.concatenate([jnp.concatenate(p, axis=1) for p in parts], axis=0)
        blocks = []
        for e in range(4):
            mk = mask_v[(4 * g + e) * 16:(4 * g + e + 1) * 16, :]
            blocks.append(lhs * jnp.concatenate([mk, mk], axis=0))
        lhs = jnp.concatenate(blocks, axis=0)
        rhs = jnp.concatenate(pair(m, g), axis=0)
        r = jnp.dot(lhs, rhs, preferred_element_type=F32)
        for e in range(4):
            for ih in range(2):
                at = (2 * e + ih) * 16
                g32[m, ih, pl.ds(4 * g + e, 16, stride=PITCH), :] = r[at:at + 16, :]

    def gather(m):
        for k in range(OWN):
            gsend[m, k * EXD:(k + 1) * EXD, :] = jnp.concatenate(
                [g32[m, ih, k * PITCH:k * PITCH + EXD, :] for ih in range(2)], axis=1
            ).astype(BF)

    def send(m):
        for i in FAR_FIRST:
            to = ahead(i)
            pltpu.make_async_remote_copy(
                src_ref=gsend.at[m, rows_of(to), :],
                dst_ref=grec.at[m, pl.ds(i * EXD, EXD), :],
                send_sem=g_send, recv_sem=g_recv.at[m if m < OUTPUT else OUTPUT + GROUP_OF[i]],
                device_id={"feat": to}, device_id_type=MESH,
            ).start()
        grec[m, 0:EXD, :] = gsend[m, rows_of(ft), :]

    def project_in(dst, source_v, weight, first, count):
        dst[first:first + count, :] = lax.dot_general(
            source_v[first:first + count, :], weight, NT, preferred_element_type=F32
        )

    ready("wnar", "gk", "gv")
    project(KEY, gk_v, wnar_v[0], 0, ROWS)
    project(VALUE, gv_v, wnar_v[1], 0, ROWS)
    ready("win", "xa0")
    win_v[3] = win_v[2]
    w_qkvv = win_v[0:4].reshape(4 * PR, D)
    project_in(pin, xa_v, w_qkvv, 0, 256)
    ready("xa1")
    project_in(pin, xa_v, w_qkvv, 256, 256)
    for g in (0, 1):
        outer(KEY, g)
        outer(VALUE, g)
    ready("wq", "gq0")
    project(QUERY, gq_v, wwide_v[0], 0, 256)
    for g in (2, 3):
        outer(KEY, g)
        outer(VALUE, g)
    gather(KEY)
    gather(VALUE)
    send(KEY)
    send(VALUE)
    ready("gq1")
    project(QUERY, gq_v, wwide_v[0], 256, 256)
    for g in (0, 1):
        outer(QUERY, g)
    ready("win3", "xc0")
    win_v[5] = win_v[4]
    w_oo = win_v[4:6].reshape(2 * PR, D)
    project_in(pin_o, xc_v, w_oo, 0, 256)
    for g in (2, 3):
        outer(QUERY, g)
    gather(QUERY)
    send(QUERY)
    ready("xc1")
    project_in(pin_o, xc_v, w_oo, 256, 256)
    ready("wo", "go0")
    project(OUTPUT, go_v, wwide_v[1], 0, 256)
    ready("go1")
    project(OUTPUT, go_v, wwide_v[1], 256, 128)
    for g in (0, 1):
        outer(OUTPUT, g)
    ready("go2")
    project(OUTPUT, go_v, wwide_v[1], 384, 128)
    outer(OUTPUT, 2)
    outer(OUTPUT, 3)
    gather(OUTPUT)
    send(OUTPUT)

    others = (OWN - 1) * EXD

    def products(m, rows):
        got = grec[m, rows, :]
        raw = lax.dot_general(got, pall[m], NT, preferred_element_type=F32)
        own = jnp.dot(got, hb_v[m], preferred_element_type=F32) * got.astype(F32)
        return raw, own[:, 0:128] + own[:, 128:256]

    arrived(pall.at[:, pl.ds(0, QN - QL), :], p_recv)
    for m in (KEY, VALUE, QUERY):
        arrived(grec.at[m, pl.ds(0, others), :], g_recv.at[m])
        raw, own = products(m, slice(0, OWN * EXD))
        if m == KEY:
            acc[...] = raw
            tacc[...] = own
        else:
            acc[...] += raw
            tacc[...] += own

    for n, group in enumerate(GROUPS):
        partners = [i for i in group if i > 0]
        arrived(grec.at[OUTPUT, pl.ds(0, len(partners) * EXD), :], g_recv.at[OUTPUT + n])
        rows = slice(group[0] * EXD, (group[-1] + 1) * EXD)
        raw, own = products(OUTPUT, rows)
        raw = raw + acc[rows, :]
        own = own + tacc[rows, :]
        own = own + pltpu.roll(own, 64, axis=1)
        high = own.astype(BF).astype(F32)
        left = lax.broadcasted_iota(jnp.int32, own.shape, 1) < 64
        sbuf[rows, 0:QN] = raw.astype(BF)
        sbuf[rows, QN:W] = jnp.where(left, high, own - high).astype(BF)
        for i in partners:
            at = pl.ds(i * EXD, EXD)
            pltpu.make_async_remote_copy(
                src_ref=sbuf.at[at, :], dst_ref=srec.at[at, :], send_sem=s_send,
                recv_sem=s_recv.at[n], device_id={"feat": behind(i)}, device_id_type=MESH,
            ).start()

    total = sbuf[0:EXD, :].astype(F32)
    for n, group in enumerate(GROUPS):
        partners = [i for i in group if i > 0]
        arrived(srec.at[pl.ds(0, len(partners) * EXD), :], s_recv.at[n])
        for i in partners:
            total = total + srec[i * EXD:(i + 1) * EXD, :].astype(F32)
    self_inf = jnp.sum(total[:, QN:W], axis=1, keepdims=True)
    out_ref[...] = total[:, 0:QN] * lax.rsqrt(self_inf + 1e-06)

    arrived(gsend.at[:, pl.ds(0, others), :], g_send)
    arrived(sbuf.at[pl.ds(0, others), :], s_send)
    arrived(pall.at[:, pl.ds(0, QN - QL), :], p_send)


def per_device(
    lengths, attn_in, context, grad_q, grad_k, grad_v, grad_o,
    proj_in, proj_out_wide, proj_out_narrow, inv_hessian, query_feats,
):
    def flat(x):
        return x.reshape(ROWS, x.shape[-1])

    any_space = pl.BlockSpec(memory_space=pl.ANY)
    dma = pltpu.SemaphoreType.DMA
    return pl.pallas_call(
        kernel,
        out_shape=jax.ShapeDtypeStruct((EXD, QN), F32),
        in_specs=[pl.BlockSpec(memory_space=pltpu.SMEM)] + [any_space] * 11,
        out_specs=pl.BlockSpec(memory_space=pltpu.VMEM),
        scratch_shapes=[
            pltpu.VMEM((ROWS, D), BF),
            pltpu.VMEM((ROWS, D), BF),
            pltpu.VMEM((ROWS, D), BF),
            pltpu.VMEM((ROWS, KVW), BF),
            pltpu.VMEM((ROWS, KVW), BF),
            pltpu.VMEM((ROWS, D), BF),
            pltpu.VMEM((6, PR, D), BF),
            pltpu.VMEM((2, PR, D), BF),
            pltpu.VMEM((2, PR, KVW), BF),
            pltpu.VMEM((4, HB, HB), F32),
            pltpu.VMEM((QL, 4, HB), F32),
            pltpu.VMEM((4, HB, HB), BF),
            pltpu.VMEM((4, QL, HB), BF),
            pltpu.VMEM((4, QN, HB), BF),
            pltpu.VMEM((ROWS, 256), F32),
            pltpu.VMEM((ROWS, 128), F32),
            pltpu.VMEM((4, EXD // 4, PR, 128), F32),
            pltpu.VMEM((EXD * 16, 256), BF),
            pltpu.VMEM((4, 2, OWN * PITCH, 128), F32),
            pltpu.VMEM((4, OWN * EXD, HB), BF),
            pltpu.VMEM((4, OWN * EXD, HB), BF),
            pltpu.VMEM((OWN * EXD, QN), F32),
            pltpu.VMEM((OWN * EXD, 128), F32),
            pltpu.VMEM((OWN * EXD, W), BF),
            pltpu.VMEM((OWN * EXD, W), BF),
            dma((18,)),
            dma,
            dma,
            dma,
            dma((OUTPUT + len(GROUPS),)),
            dma,
            dma((len(GROUPS),)),
        ],
        compiler_params=pltpu.CompilerParams(
            collective_id=0, has_side_effects=True, vmem_limit_bytes=56 << 20
        ),
    )(
        lengths, flat(attn_in), flat(context), flat(grad_q), flat(grad_k), flat(grad_v),
        flat(grad_o), proj_in, proj_out_wide, proj_out_narrow, inv_hessian, query_feats,
    )


def solution(mesh):
    both = P(("ex", "feat"), None, None)
    in_specs = (
        P(("ex", "feat")), both, both, both, both, both, both,
        P(), P(), P(),
        P(None, "feat", None, None),
        P("ex", None, "feat"),
    )
    return jax.shard_map(
        per_device, mesh=mesh, in_specs=in_specs, out_specs=P(("ex", "feat"), None), check_vma=False
    )
```

time: 34.7 us -> 31.3 us (0.902)
  Pallas kernels: 32.9 us -> 29.4 us
    pallas_call x1, Pallas kernels: 32.9 us -> 29.4 us  [per_device(): pl.pallas_call(kernel, out_shape=jax.ShapeDtypeStruct((EXD, QN), F32), in...]
where the time goes in v2:
time: 31.3 us; the launch traced here: 30.7 us
  Pallas kernels  29.4 us (94%)
  local copies, waits for them, and re-layouts  1.32 us (4%)
    pallas_call x1, Pallas kernels, per_device(): pl.pallas_call(kernel, out_shape=jax.ShapeDtypeStruct((EXD, QN), F32), in...  29.4 us
    unnamed x1, local copies, waits for them, and re-layouts  1.32 us

profile of v2, /device:TPU:1, one launch (start us, length us, event | category | flops | bytes accessed | tf_op | source)
XLA Modules:
  0.0 30.7 jit_solution(2566821113547131218)
XLA Ops:
  0.0 29.4 %shard_map.118 = f32[16,256]{1,0:T(8,128)} custom-call(s32[16]{0:T(128)} %len_ref.1, bf16[512,4096]{1,0:T(8,128)(2,1)} %bitcast.6, bf16[512,4096]{1,0:T(8,128)(2,1)} %bitcast.7, bf16[512,4096]{1,0:T(8,128)(2,1)} %bitcast.8, bf16[512,1024]{1,0:T(8,128)(2,1)} %bitcast.10, bf16[512,1024]{1,0:T(8,128)(2,1)} %bitcast.11, bf16[512,4096]{1,0:T(8,128)(2,1)} %bitcast.9, ...), custom_call_target="tpu_custom_call" | custom-call | tf_op jit(solution)/shard_map/pallas_call | solution.py:312
  29.4 1.3 %copy.14 = f32[16,256]{1,0:T(8,128)} copy(f32[16,256]{1,0:T(8,128)} %shard_map.118) | data formatting | bytes 32768

commit v3 on v2

--- a/solution.py
+++ b/solution.py
@@ -23,6 +23,7 @@
 QL = 32
 QN = 256
 W = 384
+RC = 256
 PITCH = 17
 QUERY, KEY, VALUE, OUTPUT = range(4)
 
@@ -43,8 +44,8 @@
 
 
 def kernel(
-    len_ref, xa, xc, gq, gk, gv, go, win, wwide, wnar, hes, qry, out_ref,
-    xa_v, xc_v, gq_v, gk_v, gv_v, go_v, win_v, wwide_v, wnar_v, hes_v, qry_v,
+    lengths, xa, xc, gq, gk, gv, go, win, wwide, wnar, hes, qry, out_ref,
+    len_ref, xa_v, xc_v, gq_v, gk_v, gv_v, go_v, win_v, wwide_v, wnar_v, hes_v, qry_v,
     hb_v, ploc, pall, pin, pin_o, ot, mask_v, g32, gsend, grec, acc, tacc, sbuf, srec,
     load_sem, p_send, p_recv, g_send, g_recv, s_send, s_recv,
 ):
@@ -73,47 +74,60 @@
             loads[name].wait()
             waited.add(name)
 
-    def load_rows(name, src, dst, at, size):
-        load(name, src.at[pl.ds(at, size)], dst.at[pl.ds(at, size)])
-
+    first_sem = {}
+
+    def load_wide(name, src, dst):
+        first_sem[name] = len(loads)
+        for c in range(ROWS // RC):
+            rows = pl.ds(c * RC, RC)
+            load(f"{name}{c}", src.at[rows, :], dst.at[rows, :])
+
+    def over_chunks(name, src, dst, body):
+        waited.update(f"{name}{c}" for c in range(ROWS // RC))
+
+        @pl.loop(0, ROWS // RC)
+        def _(c):
+            rows = pl.ds(pl.multiple_of(c * RC, RC), RC)
+            pltpu.make_async_copy(
+                src.at[rows, :], dst.at[rows, :], load_sem.at[first_sem[name] + c]
+            ).wait()
+            body(c, rows)
+
+    load("len", lengths, len_ref)
     load("hes", hes.at[:, 0], hes_v)
     load("qry", qry, qry_v)
     load("wnar", wnar, wnar_v)
     load("gk", gk, gk_v)
     load("gv", gv, gv_v)
-    load("win", win.at[pl.ds(0, 3)], win_v.at[pl.ds(0, 3)])
-    load_rows("xa0", xa, xa_v, 0, 256)
-    load_rows("xa1", xa, xa_v, 256, 256)
+    for m in range(3):
+        load(f"win{m}", win.at[m], win_v.at[pl.ds(m * PR, PR)])
+    load_wide("xa", xa, xa_v)
     load("wq", wwide.at[0], wwide_v.at[0])
-    load_rows("gq0", gq, gq_v, 0, 256)
-    load_rows("gq1", gq, gq_v, 256, 256)
-    load("win3", win.at[3], win_v.at[4])
-    load_rows("xc0", xc, xc_v, 0, 256)
-    load_rows("xc1", xc, xc_v, 256, 256)
+    load_wide("gq", gq, gq_v)
+    load("win3", win.at[3], win_v.at[pl.ds(4 * PR, PR)])
+    load_wide("xc", xc, xc_v)
     load("wo", wwide.at[1], wwide_v.at[1])
-    load_rows("go0", go, go_v, 0, 256)
-    load_rows("go1", go, go_v, 256, 128)
-    load_rows("go2", go, go_v, 384, 128)
+    load_wide("go", go, go_v)
 
     barrier = pltpu.get_barrier_semaphore()
-    for i in FAR_FIRST:
-        pl.semaphore_signal(barrier, inc=1, device_id={"feat": ahead(i)}, device_id_type=MESH)
-    for s in range(1, EXN):
+
+    @pl.loop(1, OWN)
+    def _(s):
+        to = ((fy + s // SIDE) % SIDE) * SIDE + (fx + s % SIDE) % SIDE
+        pl.semaphore_signal(barrier, inc=1, device_id={"feat": to}, device_id_type=MESH)
+
+    @pl.loop(1, EXN)
+    def _(s):
         pl.semaphore_signal(barrier, inc=1, device_id={"ex": (ex + s) % EXN}, device_id_type=MESH)
-
-    lane = lax.broadcasted_iota(jnp.int32, (16, 256), 1)
-    lane_e = (lane // LEN) % 4
-    lane_t = lane % LEN
-    for e in range(EXD):
-        on = (lane_e == e % 4) & (lane_t < len_ref[e])
-        mask_v[e * 16:(e + 1) * 16, :] = jnp.where(on, 1.0, 0.0).astype(BF)
 
     def halves(x):
         high = x.astype(BF)
         return high, (x - high.astype(F32)).astype(BF)
 
     ready("hes", "qry")
-    for m in range(4):
+
+    @pl.loop(0, 4)
+    def _(m):
         q_high, q_low = halves(qry_v[:, m, :])
         h_high, h_low = halves(hes_v[m])
         hb_v[m] = h_high
@@ -126,7 +140,9 @@
     pl.semaphore_wait(barrier, OWN - 1 + EXN - 1)
 
     my_q = pl.ds(pl.multiple_of(ex * QL, QL), QL)
-    for s in range(1, EXN):
+
+    @pl.loop(1, EXN)
+    def _(s):
         pltpu.make_async_remote_copy(
             src_ref=ploc, dst_ref=pall.at[:, my_q, :], send_sem=p_send, recv_sem=p_recv,
             device_id={"ex": (ex + s) % EXN}, device_id_type=MESH,
@@ -138,12 +154,13 @@
     def rows_of(k):
         return pl.ds(pl.multiple_of(k * EXD, EXD), EXD)
 
-    def project(m, target_v, weight, first, count):
+    def project(m, target_v, weight, c, rows):
         o_t = lax.dot_general(
-            weight, target_v[first:first + count, :], NT, preferred_element_type=F32
+            weight[...], target_v[rows, :], NT, preferred_element_type=F32
         )
-        for b in range(count // 128):
-            ot[m, first // 128 + b] = o_t[:, b * 128:(b + 1) * 128]
+        count = o_t.shape[1] // 128
+        for b in range(count):
+            ot[m, c * count + b] = o_t[:, b * 128:(b + 1) * 128]
 
     def split(x, left, twice):
         turned = x if twice else pltpu.roll(x, PR, axis=1)
@@ -168,7 +185,7 @@
         lhs = jnp.concatenate([jnp.concatenate(p, axis=1) for p in parts], axis=0)
         blocks = []
         for e in range(4):
-            mk = mask_v[(4 * g + e) * 16:(4 * g + e + 1) * 16, :]
+            mk = mask_v[4 * g + e]
             blocks.append(lhs * jnp.concatenate([mk, mk], axis=0))
         lhs = jnp.concatenate(blocks, axis=0)
         rhs = jnp.concatenate(pair(m, g), axis=0)
@@ -195,56 +212,46 @@
             ).start()
         grec[m, 0:EXD, :] = gsend[m, rows_of(ft), :]
 
-    def project_in(dst, source_v, weight, first, count):
-        dst[first:first + count, :] = lax.dot_general(
-            source_v[first:first + count, :], weight, NT, preferred_element_type=F32
+    def project_in(dst, source_v, weight, rows):
+        dst[rows, :] = lax.dot_general(
+            source_v[rows, :], weight[...], NT, preferred_element_type=F32
         )
 
+    every = pl.ds(0, ROWS)
+    ready("len")
+    lane = lax.broadcasted_iota(jnp.int32, (16, 256), 1)
+    lane_e = (lane // LEN) % 4
+    lane_t = lane % LEN
+
+    @pl.loop(0, EXD)
+    def _(e):
+        on = (lane_e == e % 4) & (lane_t < len_ref[e])
+        mask_v[e] = jnp.where(on, 1.0, 0.0).astype(BF)
+
     ready("wnar", "gk", "gv")
-    project(KEY, gk_v, wnar_v[0], 0, ROWS)
-    project(VALUE, gv_v, wnar_v[1], 0, ROWS)
-    ready("win", "xa0")
-    win_v[3] = win_v[2]
-    w_qkvv = win_v[0:4].reshape(4 * PR, D)
-    project_in(pin, xa_v, w_qkvv, 0, 256)
-    ready("xa1")
-    project_in(pin, xa_v, w_qkvv, 256, 256)
-    for g in (0, 1):
-        outer(KEY, g)
-        outer(VALUE, g)
-    ready("wq", "gq0")
-    project(QUERY, gq_v, wwide_v[0], 0, 256)
-    for g in (2, 3):
-        outer(KEY, g)
-        outer(VALUE, g)
-    gather(KEY)
-    gather(VALUE)
-    send(KEY)
-    send(VALUE)
-    ready("gq1")
-    project(QUERY, gq_v, wwide_v[0], 256, 256)
-    for g in (0, 1):
-        outer(QUERY, g)
-    ready("win3", "xc0")
-    win_v[5] = win_v[4]
-    w_oo = win_v[4:6].reshape(2 * PR, D)
-    project_in(pin_o, xc_v, w_oo, 0, 256)
-    for g in (2, 3):
+    project(KEY, gk_v, wnar_v.at[0], 0, every)
+    project(VALUE, gv_v, wnar_v.at[1], 0, every)
+    ready("win0", "win1", "win2")
+    win_v[3 * PR:4 * PR, :] = win_v[2 * PR:3 * PR, :]
+    over_chunks("xa", xa, xa_v, lambda c, rows: project_in(pin, xa_v, win_v.at[0:4 * PR], rows))
+    for m in (KEY, VALUE):
+        for g in range(EXD // 4):
+            outer(m, g)
+        gather(m)
+        send(m)
+    ready("wq")
+    over_chunks("gq", gq, gq_v, lambda c, rows: project(QUERY, gq_v, wwide_v.at[0], c, rows))
+    for g in range(EXD // 4):
         outer(QUERY, g)
     gather(QUERY)
     send(QUERY)
-    ready("xc1")
-    project_in(pin_o, xc_v, w_oo, 256, 256)
-    ready("wo", "go0")
-    project(OUTPUT, go_v, wwide_v[1], 0, 256)
-    ready("go1")
-    project(OUTPUT, go_v, wwide_v[1], 256, 128)
-    for g in (0, 1):
+    ready("win3")
+    win_v[5 * PR:6 * PR, :] = win_v[4 * PR:5 * PR, :]
+    over_chunks("xc", xc, xc_v, lambda c, rows: project_in(pin_o, xc_v, win_v.at[4 * PR:6 * PR], rows))
+    ready("wo")
+    over_chunks("go", go, go_v, lambda c, rows: project(OUTPUT, go_v, wwide_v.at[1], c, rows))
+    for g in range(EXD // 4):
         outer(OUTPUT, g)
-    ready("go2")
-    project(OUTPUT, go_v, wwide_v[1], 384, 128)
-    outer(OUTPUT, 2)
-    outer(OUTPUT, 3)
     gather(OUTPUT)
     send(OUTPUT)
 
@@ -312,16 +319,17 @@
     return pl.pallas_call(
         kernel,
         out_shape=jax.ShapeDtypeStruct((EXD, QN), F32),
-        in_specs=[pl.BlockSpec(memory_space=pltpu.SMEM)] + [any_space] * 11,
+        in_specs=[any_space] * 12,
         out_specs=pl.BlockSpec(memory_space=pltpu.VMEM),
         scratch_shapes=[
+            pltpu.SMEM((EXD,), jnp.int32),
             pltpu.VMEM((ROWS, D), BF),
             pltpu.VMEM((ROWS, D), BF),
             pltpu.VMEM((ROWS, D), BF),
             pltpu.VMEM((ROWS, KVW), BF),
             pltpu.VMEM((ROWS, KVW), BF),
             pltpu.VMEM((ROWS, D), BF),
-            pltpu.VMEM((6, PR, D), BF),
+            pltpu.VMEM((6 * PR, D), BF),
             pltpu.VMEM((2, PR, D), BF),
             pltpu.VMEM((2, PR, KVW), BF),
             pltpu.VMEM((4, HB, HB), F32),
@@ -332,7 +340,7 @@
             pltpu.VMEM((ROWS, 256), F32),
             pltpu.VMEM((ROWS, 128), F32),
             pltpu.VMEM((4, EXD // 4, PR, 128), F32),
-            pltpu.VMEM((EXD * 16, 256), BF),
+            pltpu.VMEM((EXD, 16, 256), BF),
             pltpu.VMEM((4, 2, OWN * PITCH, 128), F32),
             pltpu.VMEM((4, OWN * EXD, HB), BF),
             pltpu.VMEM((4, OWN * EXD, HB), BF),
@@ -340,7 +348,7 @@
             pltpu.VMEM((OWN * EXD, 128), F32),
             pltpu.VMEM((OWN * EXD, W), BF),
             pltpu.VMEM((OWN * EXD, W), BF),
-            dma((18,)),
+            dma((20,)),
             dma,
             dma,
             dma,

time: 31.3 us -> 27.7 us (0.88)
  Pallas kernels: 29.4 us -> 25.8 us
    pallas_call x1, Pallas kernels: 29.4 us -> 25.8 us  [per_device(): pl.pallas_call(kernel, out_shape=jax.ShapeDtypeStruct((EXD, QN), F32), in...]
where the time goes in v3:
time: 27.7 us; the launch traced here: 27.2 us
  Pallas kernels  25.8 us (93%)
  local copies, waits for them, and re-layouts  1.32 us (5%)
    pallas_call x1, Pallas kernels, per_device(): pl.pallas_call(kernel, out_shape=jax.ShapeDtypeStruct((EXD, QN), F32), in...  25.8 us
    unnamed x1, local copies, waits for them, and re-layouts  1.32 us

profile of v3, /device:TPU:1, one launch (start us, length us, event | category | flops | bytes accessed | tf_op | source)
XLA Modules:
  0.0 27.2 jit_solution(3748225207946224302)
XLA Ops:
  0.0 25.8 %shard_map.118 = f32[16,256]{1,0:T(8,128)} custom-call(s32[16]{0:T(128)} %lengths.1, bf16[512,4096]{1,0:T(8,128)(2,1)} %bitcast.6, bf16[512,4096]{1,0:T(8,128)(2,1)} %bitcast.7, bf16[512,4096]{1,0:T(8,128)(2,1)} %bitcast.8, bf16[512,1024]{1,0:T(8,128)(2,1)} %bitcast.10, bf16[512,1024]{1,0:T(8,128)(2,1)} %bitcast.11, bf16[512,4096]{1,0:T(8,128)(2,1)} %bitcast.9, ...), custom_call_target="tpu_custom_call" | custom-call | tf_op jit(solution)/shard_map/pallas_call | solution.py:319
  25.8 1.3 %copy.14 = f32[16,256]{1,0:T(8,128)} copy(f32[16,256]{1,0:T(8,128)} %shard_map.118) | data formatting | bytes 32768

commit v4 on v3

--- a/solution.py
+++ b/solution.py
@@ -51,15 +51,16 @@
 ):
     ex = lax.axis_index("ex")
     ft = lax.axis_index("feat")
-    fy, fx = ft // SIDE, ft % SIDE
+    xs = [(ft % SIDE + d) % SIDE for d in range(SIDE)]
+    ys = [((ft // SIDE + d) % SIDE) * SIDE for d in range(SIDE)]
 
     def ahead(i):
         dy, dx = divmod(SLOTS[i], SIDE)
-        return ((fy + dy) % SIDE) * SIDE + (fx + dx) % SIDE
+        return ys[dy] + xs[dx]
 
     def behind(i):
         dy, dx = divmod(SLOTS[i], SIDE)
-        return ((fy + SIDE - dy) % SIDE) * SIDE + (fx + SIDE - dx) % SIDE
+        return ys[-dy % SIDE] + xs[-dx % SIDE]
 
     loads = {}
     waited = set()
@@ -81,6 +82,10 @@
         for c in range(ROWS // RC):
             rows = pl.ds(c * RC, RC)
             load(f"{name}{c}", src.at[rows, :], dst.at[rows, :])
+
+    def all_rows_of(name, body):
+        ready(f"{name}0", f"{name}1")
+        body(0, pl.ds(0, ROWS))
 
     def over_chunks(name, src, dst, body):
         waited.update(f"{name}{c}" for c in range(ROWS // RC))
@@ -111,14 +116,10 @@
 
     barrier = pltpu.get_barrier_semaphore()
 
-    @pl.loop(1, OWN)
-    def _(s):
-        to = ((fy + s // SIDE) % SIDE) * SIDE + (fx + s % SIDE) % SIDE
-        pl.semaphore_signal(barrier, inc=1, device_id={"feat": to}, device_id_type=MESH)
-
-    @pl.loop(1, EXN)
-    def _(s):
-        pl.semaphore_signal(barrier, inc=1, device_id={"ex": (ex + s) % EXN}, device_id_type=MESH)
+    for d in range(1, EXN):
+        pl.semaphore_signal(barrier, inc=1, device_id={"ex": (ex + d) % EXN}, device_id_type=MESH)
+    for i in FAR_FIRST:
+        pl.semaphore_signal(barrier, inc=1, device_id={"feat": ahead(i)}, device_id_type=MESH)
 
     def halves(x):
         high = x.astype(BF)
@@ -137,16 +138,20 @@
         rest = jnp.dot(q_high, h_low, preferred_element_type=F32)
         ploc[m] = (both[0:QL] + (both[QL:2 * QL] + rest)).astype(BF)
 
-    pl.semaphore_wait(barrier, OWN - 1 + EXN - 1)
-
     my_q = pl.ds(pl.multiple_of(ex * QL, QL), QL)
 
-    @pl.loop(1, EXN)
-    def _(s):
-        pltpu.make_async_remote_copy(
-            src_ref=ploc, dst_ref=pall.at[:, my_q, :], send_sem=p_send, recv_sem=p_recv,
-            device_id={"ex": (ex + s) % EXN}, device_id_type=MESH,
-        ).start()
+    def enter():
+        pl.semaphore_wait(barrier, OWN - 1 + EXN - 1)
+
+        @pl.loop(1, EXN)
+        def _(s):
+            pltpu.make_async_remote_copy(
+                src_ref=ploc, dst_ref=pall.at[:, my_q, :], send_sem=p_send, recv_sem=p_recv,
+                device_id={"ex": (ex + s) % EXN},
+                device_id_type=MESH,
+            ).start()
+
+    late = ex >= EXN // 2
     pall[:, my_q, :] = ploc[...]
 
     half = lax.broadcasted_iota(jnp.int32, (128, 128), 1) < PR
@@ -231,23 +236,25 @@
     ready("wnar", "gk", "gv")
     project(KEY, gk_v, wnar_v.at[0], 0, every)
     project(VALUE, gv_v, wnar_v.at[1], 0, every)
+    pl.when(late)(enter)
     ready("win0", "win1", "win2")
     win_v[3 * PR:4 * PR, :] = win_v[2 * PR:3 * PR, :]
     over_chunks("xa", xa, xa_v, lambda c, rows: project_in(pin, xa_v, win_v.at[0:4 * PR], rows))
+    pl.when(jnp.logical_not(late))(enter)
     for m in (KEY, VALUE):
         for g in range(EXD // 4):
             outer(m, g)
         gather(m)
         send(m)
     ready("wq")
-    over_chunks("gq", gq, gq_v, lambda c, rows: project(QUERY, gq_v, wwide_v.at[0], c, rows))
+    all_rows_of("gq", lambda c, rows: project(QUERY, gq_v, wwide_v.at[0], c, rows))
     for g in range(EXD // 4):
         outer(QUERY, g)
     gather(QUERY)
     send(QUERY)
     ready("win3")
     win_v[5 * PR:6 * PR, :] = win_v[4 * PR:5 * PR, :]
-    over_chunks("xc", xc, xc_v, lambda c, rows: project_in(pin_o, xc_v, win_v.at[4 * PR:6 * PR], rows))
+    all_rows_of("xc", lambda c, rows: project_in(pin_o, xc_v, win_v.at[4 * PR:6 * PR], rows))
     ready("wo")
     over_chunks("go", go, go_v, lambda c, rows: project(OUTPUT, go_v, wwide_v.at[1], c, rows))
     for g in range(EXD // 4):
@@ -257,30 +264,31 @@
 
     others = (OWN - 1) * EXD
 
-    def products(m, rows):
+    def raw_part(m, rows):
+        return lax.dot_general(grec[m, rows, :], pall[m], NT, preferred_element_type=F32)
+
+    def self_part(m, rows):
         got = grec[m, rows, :]
-        raw = lax.dot_general(got, pall[m], NT, preferred_element_type=F32)
         own = jnp.dot(got, hb_v[m], preferred_element_type=F32) * got.astype(F32)
-        return raw, own[:, 0:128] + own[:, 128:256]
-
+        return own[:, 0:128] + own[:, 128:256]
+
+    early = (KEY, VALUE, QUERY)
+    all_rows = slice(0, OWN * EXD)
+    for m in early:
+        arrived(grec.at[m, pl.ds(0, others), :], g_recv.at[m])
+        own = self_part(m, all_rows)
+        tacc[...] = own if m == KEY else tacc[...] + own
     arrived(pall.at[:, pl.ds(0, QN - QL), :], p_recv)
-    for m in (KEY, VALUE, QUERY):
-        arrived(grec.at[m, pl.ds(0, others), :], g_recv.at[m])
-        raw, own = products(m, slice(0, OWN * EXD))
-        if m == KEY:
-            acc[...] = raw
-            tacc[...] = own
-        else:
-            acc[...] += raw
-            tacc[...] += own
+    for m in early:
+        raw = raw_part(m, all_rows)
+        acc[...] = raw if m == KEY else acc[...] + raw
 
     for n, group in enumerate(GROUPS):
         partners = [i for i in group if i > 0]
         arrived(grec.at[OUTPUT, pl.ds(0, len(partners) * EXD), :], g_recv.at[OUTPUT + n])
         rows = slice(group[0] * EXD, (group[-1] + 1) * EXD)
-        raw, own = products(OUTPUT, rows)
-        raw = raw + acc[rows, :]
-        own = own + tacc[rows, :]
+        raw = raw_part(OUTPUT, rows) + acc[rows, :]
+        own = self_part(OUTPUT, rows) + tacc[rows, :]
         own = own + pltpu.roll(own, 64, axis=1)
         high = own.astype(BF).astype(F32)
         left = lax.broadcasted_iota(jnp.int32, own.shape, 1) < 64

time: 27.7 us -> 25.8 us (0.931); the launches traced: 27.2 us -> 25.6 us
  Pallas kernels: 25.8 us -> 24.3 us
    pallas_call x1, Pallas kernels: 25.8 us -> 24.3 us  [per_device(): pl.pallas_call(kernel, out_shape=jax.ShapeDtypeStruct((EXD, QN), F32), in...]
where the time goes in v4:
time: 25.8 us; the launch traced here: 25.6 us
  Pallas kernels  24.3 us (94%)
  local copies, waits for them, and re-layouts  1.32 us (5%)
    pallas_call x1, Pallas kernels, per_device(): pl.pallas_call(kernel, out_shape=jax.ShapeDtypeStruct((EXD, QN), F32), in...  24.3 us
    unnamed x1, local copies, waits for them, and re-layouts  1.32 us

profile of v4, /device:TPU:1, one launch (start us, length us, event | category | flops | bytes accessed | tf_op | source)
XLA Modules:
  0.0 25.6 jit_solution(6704913431521857293)
XLA Ops:
  0.0 24.3 %shard_map.118 = f32[16,256]{1,0:T(8,128)} custom-call(s32[16]{0:T(128)} %lengths.1, bf16[512,4096]{1,0:T(8,128)(2,1)} %bitcast.6, bf16[512,4096]{1,0:T(8,128)(2,1)} %bitcast.7, bf16[512,4096]{1,0:T(8,128)(2,1)} %bitcast.8, bf16[512,1024]{1,0:T(8,128)(2,1)} %bitcast.10, bf16[512,1024]{1,0:T(8,128)(2,1)} %bitcast.11, bf16[512,4096]{1,0:T(8,128)(2,1)} %bitcast.9, ...), custom_call_target="tpu_custom_call" | custom-call | tf_op jit(solution)/shard_map/pallas_call | solution.py:327
  24.3 1.3 %copy.14 = f32[16,256]{1,0:T(8,128)} copy(f32[16,256]{1,0:T(8,128)} %shard_map.118) | data formatting | bytes 32768

commit v5 on v4

--- a/solution.py
+++ b/solution.py
@@ -143,11 +143,12 @@
     def enter():
         pl.semaphore_wait(barrier, OWN - 1 + EXN - 1)
 
-        @pl.loop(1, EXN)
+        @pl.loop(0, EXN - 1)
         def _(s):
+            to = jnp.where(s < ex, s, s + 1)
             pltpu.make_async_remote_copy(
                 src_ref=ploc, dst_ref=pall.at[:, my_q, :], send_sem=p_send, recv_sem=p_recv,
-                device_id={"ex": (ex + s) % EXN},
+                device_id={"ex": to},
                 device_id_type=MESH,
             ).start()
 
@@ -294,12 +295,12 @@
         left = lax.broadcasted_iota(jnp.int32, own.shape, 1) < 64
         sbuf[rows, 0:QN] = raw.astype(BF)
         sbuf[rows, QN:W] = jnp.where(left, high, own - high).astype(BF)
-        for i in partners:
-            at = pl.ds(i * EXD, EXD)
-            pltpu.make_async_remote_copy(
-                src_ref=sbuf.at[at, :], dst_ref=srec.at[at, :], send_sem=s_send,
-                recv_sem=s_recv.at[n], device_id={"feat": behind(i)}, device_id_type=MESH,
-            ).start()
+    for i in FAR_FIRST:
+        at = pl.ds(i * EXD, EXD)
+        pltpu.make_async_remote_copy(
+            src_ref=sbuf.at[at, :], dst_ref=srec.at[at, :], send_sem=s_send,
+            recv_sem=s_recv.at[GROUP_OF[i]], device_id={"feat": behind(i)}, device_id_type=MESH,
+        ).start()
 
     total = sbuf[0:EXD, :].astype(F32)
     for n, group in enumerate(GROUPS):
@@ -326,7 +327,7 @@
     dma = pltpu.SemaphoreType.DMA
     return pl.pallas_call(
         kernel,
-        out_shape=jax.ShapeDtypeStruct((EXD, QN), F32),
+        out_shape=pltpu.VMEM((EXD, QN), F32),
         in_specs=[any_space] * 12,
         out_specs=pl.BlockSpec(memory_space=pltpu.VMEM),
         scratch_shapes=[

time: 25.8 us -> 23.9 us (0.926)
  Pallas kernels: 24.3 us -> 23 us
  local copies, waits for them, and re-layouts: 1.32 us -> 0.61 us
    pallas_call x1, Pallas kernels: 24.3 us -> 23 us  [per_device(): pl.pallas_call(kernel, out_shape=pltpu.VMEM((EXD, QN), F32), in_specs=[an...]
    unnamed x1, local copies, waits for them, and re-layouts: 1.32 us -> 0.61 us
where the time goes in v5:
time: 23.9 us; the launch traced here: 23.6 us
  Pallas kernels  23 us (96%)
  local copies, waits for them, and re-layouts  0.61 us (3%)
    pallas_call x1, Pallas kernels, per_device(): pl.pallas_call(kernel, out_shape=pltpu.VMEM((EXD, QN), F32), in_specs=[an...  23 us
    unnamed x1, local copies, waits for them, and re-layouts  0.61 us

profile of v5, /device:TPU:1, one launch (start us, length us, event | category | flops | bytes accessed | tf_op | source)
XLA Modules:
  0.0 23.6 jit_solution(16031976054422772838)
XLA Ops:
  0.0 23.0 %shard_map.118 = f32[16,256]{1,0:T(8,128)S(1)} custom-call(s32[16]{0:T(128)} %lengths.1, bf16[512,4096]{1,0:T(8,128)(2,1)} %bitcast.6, bf16[512,4096]{1,0:T(8,128)(2,1)} %bitcast.7, bf16[512,4096]{1,0:T(8,128)(2,1)} %bitcast.8, bf16[512,1024]{1,0:T(8,128)(2,1)} %bitcast.10, bf16[512,1024]{1,0:T(8,128)(2,1)} %bitcast.11, bf16[512,4096]{1,0:T(8,128)(2,1)} %bitcast.9, ...), custom_call_target="tpu_custom_call" | custom-call | tf_op jit(solution)/shard_map/pallas_call | solution.py:328
  23.0 0.6 %copy.14 = f32[16,256]{1,0:T(8,128)} copy(f32[16,256]{1,0:T(8,128)S(1)} %shard_map.118) | data formatting | bytes 32768

commit v6 on v5

--- a/solution.py
+++ b/solution.py
@@ -63,7 +63,6 @@
         return ys[-dy % SIDE] + xs[-dx % SIDE]
 
     loads = {}
-    waited = set()
 
     def load(name, src, dst):
         copy = pltpu.make_async_copy(src, dst, load_sem.at[len(loads)])
@@ -73,7 +72,6 @@
     def ready(*names):
         for name in names:
             loads[name].wait()
-            waited.add(name)
 
     first_sem = {}
 
@@ -88,8 +86,6 @@
         body(0, pl.ds(0, ROWS))
 
     def over_chunks(name, src, dst, body):
-        waited.update(f"{name}{c}" for c in range(ROWS // RC))
-
         @pl.loop(0, ROWS // RC)
         def _(c):
             rows = pl.ds(pl.multiple_of(c * RC, RC), RC)
@@ -287,14 +283,13 @@
     for n, group in enumerate(GROUPS):
         partners = [i for i in group if i > 0]
         arrived(grec.at[OUTPUT, pl.ds(0, len(partners) * EXD), :], g_recv.at[OUTPUT + n])
-        rows = slice(group[0] * EXD, (group[-1] + 1) * EXD)
-        raw = raw_part(OUTPUT, rows) + acc[rows, :]
-        own = self_part(OUTPUT, rows) + tacc[rows, :]
-        own = own + pltpu.roll(own, 64, axis=1)
-        high = own.astype(BF).astype(F32)
-        left = lax.broadcasted_iota(jnp.int32, own.shape, 1) < 64
-        sbuf[rows, 0:QN] = raw.astype(BF)
-        sbuf[rows, QN:W] = jnp.where(left, high, own - high).astype(BF)
+    raw = raw_part(OUTPUT, all_rows) + acc[...]
+    own = self_part(OUTPUT, all_rows) + tacc[...]
+    own = own + pltpu.roll(own, 64, axis=1)
+    high = own.astype(BF).astype(F32)
+    left = lax.broadcasted_iota(jnp.int32, own.shape, 1) < 64
+    sbuf[:, 0:QN] = raw.astype(BF)
+    sbuf[:, QN:W] = jnp.where(left, high, own - high).astype(BF)
     for i in FAR_FIRST:
         at = pl.ds(i * EXD, EXD)
         pltpu.make_async_remote_copy(

time: 23.9 us -> 23.7 us (level)
  the two profiles are of different devices: /device:TPU:1 before, /device:TPU:64 now
where the time goes in v6:
time: 23.7 us; the launch traced here: 23.6 us
  Pallas kernels  23 us (97%)
  local copies, waits for them, and re-layouts  0.61 us (3%)
    pallas_call x1, Pallas kernels, per_device(): pl.pallas_call(kernel, out_shape=pltpu.VMEM((EXD, QN), F32), in_specs=[an...  23 us
    unnamed x1, local copies, waits for them, and re-layouts  0.61 us

profile of v6, /device:TPU:64, one launch (start us, length us, event | category | flops | bytes accessed | tf_op | source)
XLA Modules:
  0.0 23.6 jit_solution(5123543613158364982)
XLA Ops:
  0.0 23.0 %shard_map.118 = f32[16,256]{1,0:T(8,128)S(1)} custom-call(s32[16]{0:T(128)} %lengths.1, bf16[512,4096]{1,0:T(8,128)(2,1)} %bitcast.6, bf16[512,4096]{1,0:T(8,128)(2,1)} %bitcast.7, bf16[512,4096]{1,0:T(8,128)(2,1)} %bitcast.8, bf16[512,1024]{1,0:T(8,128)(2,1)} %bitcast.10, bf16[512,1024]{1,0:T(8,128)(2,1)} %bitcast.11, bf16[512,4096]{1,0:T(8,128)(2,1)} %bitcast.9, ...), custom_call_target="tpu_custom_call" | custom-call | tf_op jit(solution)/shard_map/pallas_call | solution.py:323
  23.0 0.6 %copy.14 = f32[16,256]{1,0:T(8,128)} copy(f32[16,256]{1,0:T(8,128)S(1)} %shard_map.118) | data formatting | bytes 32768

commit v7 on v6

--- a/solution.py
+++ b/solution.py
@@ -162,7 +162,7 @@
         )
         count = o_t.shape[1] // 128
         for b in range(count):
-            ot[m, c * count + b] = o_t[:, b * 128:(b + 1) * 128]
+            ot[m, c * count + b, 0:PR, :] = o_t[:, b * 128:(b + 1) * 128]
 
     def split(x, left, twice):
         turned = x if twice else pltpu.roll(x, PR, axis=1)
@@ -343,9 +343,9 @@
             pltpu.VMEM((4, QN, HB), BF),
             pltpu.VMEM((ROWS, 256), F32),
             pltpu.VMEM((ROWS, 128), F32),
-            pltpu.VMEM((4, EXD // 4, PR, 128), F32),
+            pltpu.VMEM((4, EXD // 4, PR + 8, 128), F32),
             pltpu.VMEM((EXD, 16, 256), BF),
-            pltpu.VMEM((4, 2, OWN * PITCH, 128), F32),
+            pltpu.VMEM((4, 2, OWN * PITCH + 16, 128), F32),
             pltpu.VMEM((4, OWN * EXD, HB), BF),
             pltpu.VMEM((4, OWN * EXD, HB), BF),
             pltpu.VMEM((OWN * EXD, QN), F32),

time: 23.7 us -> 23.7 us (level)
  no operation moved by 1% of the time
where the time goes in v7:
time: 23.7 us; the launch traced here: 23.6 us
  Pallas kernels  23 us (97%)
  local copies, waits for them, and re-layouts  0.61 us (3%)
    pallas_call x1, Pallas kernels, per_device(): pl.pallas_call(kernel, out_shape=pltpu.VMEM((EXD, QN), F32), in_specs=[an...  23 us
    unnamed x1, local copies, waits for them, and re-layouts  0.61 us

profile of v7, /device:TPU:64, one launch (start us, length us, event | category | flops | bytes accessed | tf_op | source)
XLA Modules:
  0.0 23.6 jit_solution(13993226928897036351)
XLA Ops:
  0.0 23.0 %shard_map.118 = f32[16,256]{1,0:T(8,128)S(1)} custom-call(s32[16]{0:T(128)} %lengths.1, bf16[512,4096]{1,0:T(8,128)(2,1)} %bitcast.6, bf16[512,4096]{1,0:T(8,128)(2,1)} %bitcast.7, bf16[512,4096]{1,0:T(8,128)(2,1)} %bitcast.8, bf16[512,1024]{1,0:T(8,128)(2,1)} %bitcast.10, bf16[512,1024]{1,0:T(8,128)(2,1)} %bitcast.11, bf16[512,4096]{1,0:T(8,128)(2,1)} %bitcast.9, ...), custom_call_target="tpu_custom_call" | custom-call | tf_op jit(solution)/shard_map/pallas_call | solution.py:323
  23.0 0.6 %copy.14 = f32[16,256]{1,0:T(8,128)} copy(f32[16,256]{1,0:T(8,128)S(1)} %shard_map.118) | data formatting | bytes 32768
